TPU v7x, 512 devices: a whole 4x8x8 slice. The times are simulated.
512 devices in a mesh: dp: 8 (over x, core), tensor: 8 (over z), vocab: 8 (over y).
Axes of the slice: x: 4, y: 8, z: 8, core: 2. Of those that a mesh axis runs over, the one named last changes fastest.
Arguments:
- hidden_in: bfloat16 [1024, 4608], P('dp')
- norm_pre: float32 [4608], replicated, may hold values from 0.1 to 1.9
- w_gate: bfloat16 [4608, 18432], P('dp', ('tensor', 'vocab')), may hold values from -0.09375 to 0.09375
- w_up: bfloat16 [4608, 18432], P('dp', ('tensor', 'vocab')), may hold values from -0.09375 to 0.09375
- w_down: bfloat16 [18432, 4608], P(('tensor', 'vocab'), 'dp'), may hold values from -0.125 to 0.125
- norm_post: float32 [4608], replicated, may hold values from 0.1 to 1.9
- norm_final: float32 [4608], replicated, may hold values from 0.1 to 1.9
- unembed: bfloat16 [4608, 131072], P(None, ('dp', 'tensor', 'vocab')), may hold values from -0.375 to 0.375
- token_ids: int32 [1024], P('dp'), may hold values from 0 to 131071
- lengths: int32 [16], P('dp'), may hold values from 1 to 63, as said below
Outputs:
- token_logprob: float32 [1024], P('dp')
Inputs may be any that keep to these rules, and one draw needn't show every extreme that they name: The rollouts are numbered by index of dp, 2 to each; the lengths of the rollouts of one index of dp sum to at most 64, and to exactly 64 on at least one index of dp, whose rollouts have lengths 64 - 1 and 1.
All inputs are finite; a program needn't handle non-finite values.
Results may differ from a plain program's by a relative error of at most 0.0035.
Values may be sent and summed in bfloat16 or wider, within the bound.
A program may use at most 64 MiB of HBM per device.

v0:
```python
import jax
import jax.numpy as jnp
from jax import lax
from jax.sharding import PartitionSpec as P

EPS = 1e-06
CAP = 30.0


def on_device(
    hidden_in, norm_pre, w_gate, w_up, w_down, norm_post, norm_final, unembed, token_ids, lengths
):
    slot_count = hidden_in.shape[0]
    segment = slot_count // lengths.shape[0]
    position = jnp.arange(slot_count, dtype=jnp.int32)
    which = (position // segment)[:, None] == jnp.arange(lengths.shape[0], dtype=jnp.int32)[None, :]
    bounds = jnp.sum(jnp.where(which, lengths[None, :], 0), axis=1)
    scored = position % segment < bounds
    stream_in = hidden_in.astype(jnp.float32)
    normed = (
        stream_in
        * lax.rsqrt(jnp.mean(stream_in * stream_in, axis=1, keepdims=True) + EPS)
        * norm_pre
    ).astype(jnp.bfloat16)
    spread = lax.all_to_all(normed, "dp", split_axis=1, concat_axis=0, tiled=True)
    paired = jnp.concatenate([w_gate, w_up], axis=1)
    gate_up = lax.psum_scatter(
        jnp.dot(spread, paired, preferred_element_type=jnp.float32).astype(jnp.bfloat16),
        "dp",
        scatter_dimension=0,
        tiled=True,
    ).astype(jnp.float32)
    units = w_gate.shape[1]
    hidden = (jax.nn.silu(gate_up[:, :units]) * gate_up[:, units:]).astype(jnp.bfloat16)
    branch = jnp.dot(
        hidden, lax.all_gather(w_down, "dp", axis=1, tiled=True), preferred_element_type=jnp.float32
    )
    summed = lax.psum(branch, ("tensor", "vocab"))
    stream = (
        stream_in
        + summed * lax.rsqrt(jnp.mean(summed * summed, axis=1, keepdims=True) + EPS) * norm_post
    )
    final = (
        stream * lax.rsqrt(jnp.mean(stream * stream, axis=1, keepdims=True) + EPS) * norm_final
    ).astype(jnp.bfloat16)
    every_row, every_target = (
        lax.all_gather(final, "dp", axis=0, tiled=True),
        lax.all_gather(token_ids, "dp", axis=0, tiled=True),
    )
    shard = unembed.shape[1]
    offset = lax.axis_index(("dp", "tensor", "vocab")) * shard
    capped = CAP * jnp.tanh(jnp.dot(every_row, unembed, preferred_element_type=jnp.float32) / CAP)
    totals = jnp.sum(jnp.exp(capped - CAP), axis=1)
    matches = jnp.arange(shard, dtype=jnp.int32)[None, :] + offset == every_target[:, None]
    sampled = jnp.sum(jnp.where(matches, capped, 0.0), axis=1)
    every_total, every_sampled = lax.psum((totals, sampled), ("dp", "tensor", "vocab"))
    count = every_total.shape[0] // lax.axis_size("dp")
    start = lax.axis_index("dp") * count
    own_total = lax.dynamic_slice_in_dim(every_total, start, count, 0)
    own_target = lax.dynamic_slice_in_dim(every_sampled, start, count, 0)
    logprob = own_target - CAP - jnp.log(own_total)
    return jnp.where(scored, logprob, 0.0)


def solution(mesh):
    in_specs = (
        P("dp", None),
        P(),
        P("dp", ("tensor", "vocab")),
        P("dp", ("tensor", "vocab")),
        P(("tensor", "vocab"), "dp"),
        P(),
        P(),
        P(None, ("dp", "tensor", "vocab")),
        P("dp"),
        P("dp"),
    )
    out_specs = P("dp")
    return jax.shard_map(
        on_device, mesh=mesh, in_specs=in_specs, out_specs=out_specs, check_vma=False
    )
```

profile of v0, /device:TPU:6, one launch (start us, length us, event | category | flops | bytes accessed | tf_op | source)
XLA Modules:
  0.0 462.7 jit_solution(11924387753720224544)
XLA Ops:
  6.5 1.7 fusion
  8.3 2.6 fusion.2
  10.9 1.7 copy.17
  12.6 0.0 copy-start.6
  12.6 23.8 %all_to_all.19 = bf16[128,8,576]{0,2,1:T(8,128)(2,1)S(1)} all-to-all(bf16[128,8,576]{0,2,1:T(8,128)(2,1)S(1)} %bitcast.20), channel_id=1, replica_groups=mesh['dp'=8,'tensor'=8,'vocab'=8] {'dp'}, dimensions={1} | all-to-all | bytes 2359296 | tf_op jit(solution)/shard_map/all_to_all | solution.py:25
  36.5 1.1 convolution_convert_fusion
  37.5 1.4 copy.20
  39.0 0.0 reduce-scatter.4.cloned.1.call-update
  39.0 0.0 all-gather.7.cloned.1.call-start
  39.1 0.7 all-gather.7.cloned.1.call-update
  39.8 0.0 all-reduce.3.cloned.1.call-start
  39.8 34.5 %reduce-scatter.4.cloned.1.call-done = bf16[128,576]{1,0:T(8,128)(2,1)} async-done(((bf16[1024,576]{1,0:T(8,128)(2,1)}), bf16[128,576]{1,0:T(8,128)(2,1)}) %reduce-scatter.4.cloned.1.call-update) | async-done | bytes 147472
  74.3 1.1 copy.21
  75.4 34.5 %all-gather.7.cloned.1.call-done = bf16[8,576,288]{1,2,0:T(8,128)(2,1)} async-done(((bf16[1,576,288]{1,2,0:T(8,128)(2,1)}), bf16[8,576,288]{1,2,0:T(8,128)(2,1)}) %all-gather.7.cloned.1.call-update) | async-done | bytes 2654224 | tf_op jit(solution)/shard_map/all_gather | solution.py:36
  109.9 4.5 copy.19
  114.3 5.6 %reshape.53 = bf16[4608,288]{0,1:T(8,128)(2,1)} reshape(bf16[8,576,288]{1,0,2:T(8,128)(2,1)} %copy.19) | data formatting | bytes 5308416
  119.9 4.0 fusion.11
  123.9 0.0 all-reduce.3.cloned.1.call-update
  124.0 0.0 all-gather.5.cloned.1.call-start
  124.0 165.7 %all-reduce.3.cloned.1.call-done = f32[128,4608]{1,0:T(8,128)} async-done(((f32[128,4608]{1,0:T(8,128)}), f32[128,4608]{1,0:T(8,128)}) %all-reduce.3.cloned.1.call-update) | async-done | bytes 2359312 | tf_op jit(solution)/shard_map/psum | solution.py:38
  289.7 2.1 multiply_reduce_fusion.1
  291.8 0.0 copy-start.4
  291.8 0.3 copy-done.1
  292.1 1.4 multiply_reduce_fusion
  293.5 1.6 multiply_convert_fusion
  295.1 0.0 all-gather.5.cloned.1.call-update
  295.1 7.4 %all-gather = s32[8,1,128]{2,1,0:T(1,128)S(1)} all-gather(s32[1,1,128]{2,1,0:T(1,128)S(1)} %bitcast.23), channel_id=1, replica_groups=mesh['dp'=8,'tensor'=8,'vocab'=8] {'dp'}, dimensions={0}, use_global_device_ids=true | all-gather | bytes 4608 | tf_op jit(solution)/shard_map/all_gather | solution.py:48
  302.5 0.1 fusion.14
  302.6 46.7 %all-gather.5.cloned.1.call-done = bf16[1024,4608]{1,0:T(8,128)(2,1)} async-done(((bf16[128,4608]{1,0:T(8,128)(2,1)}), bf16[1024,4608]{1,0:T(8,128)(2,1)}) %all-gather.5.cloned.1.call-update) | async-done | bytes 9437200 | tf_op jit(solution)/shard_map/all_gather | solution.py:47
  349.4 6.6 %select_reduce_fusion = (f32[1024]{0:T(1024)S(1)}, f32[1024]{0:T(1024)S(1)}) fusion(s32[1024]{0:T(1024)S(1)} %bitcast.22, s32[256]{0:T(256)S(1)} %iota_add_fusion, bf16[1024,4608]{1,0:T(8,128)(2,1)} %all-gather.5.cloned.1.call-done, bf16[4608,256]{1,0:T(8,128)(2,1)S(1)} %copy-done), kind=kOutput, calls=%fused_computation.16 | convolution fusion | flops 2417752064 | bytes 11809792 | tf_op jit(solution)/shard_map/dot_general | solution.py:52
  355.9 99.7 %all-reduce = (f32[1024]{0:T(1024)S(1)}, f32[1024]{0:T(1024)S(1)}) all-reduce(f32[1024]{0:T(1024)S(1)} %get-tuple-element.6, f32[1024]{0:T(1024)S(1)} %get-tuple-element.5), channel_id=1, replica_groups=mesh['dp'=8,'tensor'=8,'vocab'=8] {'dp','tensor','vocab'}, use_global_device_ids=true, to_apply=%region_9.10 | all-reduce | flops 2048 | bytes 16384 | tf_op jit(solution)/shard_map/psum | solution.py:56
  455.6 0.6 compare_select_fusion
  (22 shorter events, 0.1 us)
Async XLA Ops:
  6.5 342.8 %copy-start = (bf16[4608,256]{1,0:T(8,128)(2,1)S(1)}, bf16[4608,256]{1,0:T(8,128)(2,1)}, u32[]{:S(2)}) copy-start(bf16[4608,256]{1,0:T(8,128)(2,1)} %param.17) | copy-start | bytes 7077892
  6.5 67.7 %reduce-scatter.4.cloned.1.call-start = ((), (), s32[]{:S(2)}) async-start(), calls=%async_computation.5 | async-start | bytes 1474560
  12.6 23.8 %copy-start.6 = (bf16[576,288]{0,1:T(8,128)(2,1)S(1)}, bf16[576,288]{0,1:T(8,128)(2,1)}, u32[]{:S(2)}) copy-start(bf16[576,288]{0,1:T(8,128)(2,1)} %param.13) | copy-start | bytes 995332
  12.6 23.8 %copy-start.7 = (bf16[576,288]{0,1:T(8,128)(2,1)S(1)}, bf16[576,288]{0,1:T(8,128)(2,1)}, u32[]{:S(2)}) copy-start(bf16[576,288]{0,1:T(8,128)(2,1)} %param.12) | copy-start | bytes 995332
  39.0 70.9 %all-gather.7.cloned.1.call-start = ((), (), s32[]{:S(2)}) async-start(), calls=%async_computation.4 | async-start | bytes 3317760 | tf_op jit(solution)/shard_map/all_gather | solution.py:36
  39.8 249.9 %all-reduce.3.cloned.1.call-start = ((), (), s32[]{:S(2)}) async-start(), calls=%async_computation.2 | async-start | bytes 4718592 | tf_op jit(solution)/shard_map/psum | solution.py:38
  123.9 167.9 %copy-start.2 = (bf16[128,4608]{1,0:T(8,128)(2,1)S(1)}, bf16[128,4608]{1,0:T(8,128)(2,1)}, u32[]{:S(2)}) copy-start(bf16[128,4608]{1,0:T(8,128)(2,1)} %param.10) | copy-start | bytes 3538948
  124.0 225.4 %all-gather.5.cloned.1.call-start = ((), (), s32[]{:S(2)}) async-start(), calls=%async_computation.3 | async-start | bytes 10616832 | tf_op jit(solution)/shard_map/all_gather | solution.py:47
  289.7 2.4 copy-start.1
  291.8 1.7 copy-start.3
  291.8 1.7 copy-start.4
  293.5 1.7 copy-start.5
  293.5 9.1 %copy-start.8 = (s32[2]{0:T(128)S(1)}, s32[2]{0:T(128)}, u32[]{:S(2)}) copy-start(s32[2]{0:T(128)} %param.19) | copy-start | bytes 28
Sparse Core Ops, SparseCore 0:
  39.1 35.0 reduce-scatter.3
  76.4 33.4 all-gather.6
  124.1 165.5 all-reduce.2
  295.3 54.0 all-gather.4
where the time goes:
time: 465 us; the launch traced here: 463 us
  waiting for transfers between devices  282 us (61%)
  blocking collectives  131 us (28%)
  local copies, waits for them, and re-layouts  14.6 us (3%)
  between operations  13.3 us (3%)
  matrix products  11.7 us (3%)
  other arithmetic  10.1 us (2%)
    psum x1, waiting for transfers between devices, on_device(): summed = lax.psum(branch, ('tensor', 'vocab'))  166 us
    psum x1, blocking collectives, on_device(): lax.psum((totals, sampled), ('dp', 'tensor', 'vocab'))  99.7 us
    all_gather x1, waiting for transfers between devices, on_device(): lax.all_gather(final, 'dp', axis=0, tiled=True)  46.7 us
    unnamed x5, waiting for transfers between devices  35.2 us
    all_gather x1, waiting for transfers between devices, on_device(): lax.all_gather(w_down, 'dp', axis=1, tiled=True)  34.5 us
    all_to_all x1, blocking collectives, on_device(): lax.all_to_all(normed, 'dp', split_axis=1, concat_axis=0, tiled=True)  23.8 us
  transfers between devices with their start and end apart: 4, of which 4 were waited for; matrix products, arithmetic and copies ran while one was open for 0% of the time, Pallas kernels for 0%

commit v1 on v0

v1 whole, which is shorter than its diff:
```python
import functools

import jax
import jax.numpy as jnp
from jax import lax
from jax.experimental import pallas as pl
from jax.experimental.pallas import tpu as pltpu
from jax.sharding import PartitionSpec as P

EPS = 1e-06
CAP = 30.0
LIVE = 64
MESH = pl.DeviceIdType.MESH
BF = jnp.bfloat16
F32 = jnp.float32
LAST = (((1,), (1,)), ((), ()))


def far_first(n):
    order = []
    for step in range(n // 2, 0, -1):
        order.append(step)
        if n - step != step:
            order.append(n - step)
    return order


def near_first(n):
    return far_first(n)[::-1]


def kernel(
    cfg,
    hid_hbm, pre_hbm, post_hbm, fin_hbm, wg_hbm, wu_hbm, wd_hbm, un_hbm, tok_hbm, len_hbm,
    out_ref,
    hid, gains, tok_ref, len_ref, hs, hx, wgu, wd2, wd, un,
    own, ps, pr, hb, bs, r1, s1, r2, st, sr, fa, fb, tk, fs, fx, fyb, fy, fzb, fz,
    l_sem, c_ssem, c_rsem, a_ssem, a_rsem, t_ssem, t_rsem, p_ssem, p_rsem, h_ssem, h_rsem,
    b1_ssem, b1_rsem, b2_ssem, b2_rsem, n_ssem, n_rsem, ga_ssem, ga_rsem, gb_ssem, gb_rsem,
    rr_ssem, rr_rsem, rl_ssem, rl_rsem, gx_ssem, gx_rsem, fx_ssem, fx_rsem, fy_ssem, fy_rsem, fz_ssem, fz_rsem,
):
    NX, NY, NZ, D, U, VS = cfg
    DC = D // NX
    DH = DC // 2
    NG = NY
    E = NG // NX
    GR = NX * LIVE // (2 * NG)
    DA = fa.shape[-1]
    TOK = hid.shape[0]
    dp = lax.axis_index("dp")
    z = lax.axis_index("tensor")
    y = lax.axis_index("vocab")
    x = dp // 2
    c = dp % 2

    def xpeer(k):
        return {"dp": lax.rem(dp + 2 * k, 2 * NX)}

    def ypeer(k):
        return {"vocab": lax.rem(y + k, NY)}

    def zpeer(k):
        return {"tensor": lax.rem(z + k, NZ)}

    core = {"dp": dp + 1 - 2 * c}
    here = (y, z)
    first = (ypeer, zpeer)
    second = (zpeer, ypeer)

    def rcopy(src, dst, ss, rs, dev):
        return pltpu.make_async_remote_copy(
            src_ref=src, dst_ref=dst, send_sem=ss, recv_sem=rs, device_id=dev, device_id_type=MESH
        )

    sent = []

    def go(copy):
        copy.start()
        sent.append(copy)
        return copy

    far_x = far_first(NX)
    near_x = near_first(NX)
    far_y = far_first(NY)

    tok_in = pltpu.make_async_copy(tok_hbm, tok_ref, l_sem.at[NX + 7])
    len_in = pltpu.make_async_copy(len_hbm, len_ref, l_sem.at[NX + 8])
    len_in.start()
    tok_in.start()
    hid_in = []
    for n, k in enumerate(far_x + [0]):
        cols = pl.ds(pl.multiple_of(lax.rem(x + k, NX) * DC, 128), DC)
        cp = pltpu.make_async_copy(hid_hbm.at[:, cols], hid.at[:, cols], l_sem.at[n])
        cp.start()
        hid_in.append((k, cols, cp))
    w_in = [
        pltpu.make_async_copy(wg_hbm, wgu.at[c, 0:U], l_sem.at[NX]),
        pltpu.make_async_copy(wu_hbm, wgu.at[c, U:2 * U], l_sem.at[NX + 1]),
        pltpu.make_async_copy(wd_hbm, wd2.at[c], l_sem.at[NX + 2]),
        pltpu.make_async_copy(un_hbm, un.at[c], l_sem.at[NX + 3]),
    ]
    for cp in w_in:
        cp.start()
    gain_in = []
    for n, src in enumerate((pre_hbm, post_hbm, fin_hbm)):
        cp = pltpu.make_async_copy(src, gains.at[n], l_sem.at[NX + 4 + n])
        cp.start()
        gain_in.append(cp)

    def gain(n):
        gain_in[n].wait()
        lines = DC // 128
        return jnp.concatenate([gains[n, pl.ds(x * lines + i, 1)] for i in range(lines)], axis=1)

    barrier = pltpu.get_barrier_semaphore()
    partners = [core] + [xpeer(k) for k in range(1, NX)] + [ypeer(k) for k in range(1, NY)] + [zpeer(k) for k in range(1, NZ)]
    for dev in partners:
        pl.semaphore_signal(barrier, inc=1, device_id=dev, device_id_type=MESH)

    len_in.wait()
    l0 = len_ref[0]
    l1 = len_ref[1]
    prow = lax.broadcasted_iota(jnp.int32, (LIVE, TOK), 0)
    scol = lax.broadcasted_iota(jnp.int32, (LIVE, TOK), 1)
    origin = jnp.where(prow < l0, prow, jnp.where(prow < l0 + l1, prow - l0 + LIVE, -1))
    pick = scol == origin
    keep = jnp.where(pick, 1.0, 0.0).astype(BF)
    eye_low = scol == prow
    eye_high = scol == prow + LIVE

    pl.semaphore_wait(barrier, len(partners))

    w_out = [
        rcopy(wg_hbm, wgu.at[c, 0:U], c_ssem.at[0], c_rsem.at[0], core),
        rcopy(wu_hbm, wgu.at[c, U:2 * U], c_ssem.at[1], c_rsem.at[1], core),
        rcopy(wd_hbm, wd2.at[c], c_ssem.at[2], c_rsem.at[2], core),
        rcopy(un_hbm, un.at[c], c_ssem.at[3], c_rsem.at[3], core),
    ]
    go(w_out[0])
    go(w_out[1])

    square = jnp.zeros((LIVE, 1), F32)
    a_cp = {}
    for k, cols, cp in hid_in:
        cp.wait()
        part = jnp.dot(keep, hid[:, cols], preferred_element_type=F32)
        cut = part.astype(BF)
        if k == 0:
            for q in range(2 * E):
                hx[x, q] = cut[q * GR:(q + 1) * GR]
        else:
            for q in range(2 * E):
                hs[k - 1, q] = cut[q * GR:(q + 1) * GR]
            a_cp[k] = go(rcopy(hs.at[k - 1], hx.at[x], a_ssem.at[k - 1], a_rsem.at[k - 1], xpeer(k)))
        square = square + jnp.sum(part * part, axis=1, keepdims=True)
    go(w_out[2])
    go(w_out[3])
    scale = lax.rsqrt(square / D + EPS)

    tok_in.wait()
    toks = jnp.sum(jnp.where(pick, tok_ref[...].astype(F32), 0.0), axis=1, keepdims=True)
    tok_row = jnp.sum(jnp.where(eye_low, toks, 0.0), axis=0, keepdims=True)
    tk[x] = jnp.broadcast_to(tok_row, (8, TOK))
    t_cp = {}
    for k in range(1, NX):
        t_cp[k] = go(rcopy(tk.at[x], tk.at[x], t_ssem.at[k - 1], t_rsem.at[k - 1], xpeer(k)))

    gain_pre = gain(0)
    for n in range(2):
        w_in[n].wait()
        w_out[n].wait_recv()
    p_cp = {}
    for k in [0] + near_x:
        j = lax.rem(x - k + NX, NX)
        if k:
            a_cp[k].wait_recv()
        rows = hx[j].reshape(LIVE, DC).astype(F32)
        rows = (rows * gain_pre).astype(BF)
        part = lax.dot_general(rows[:, 0:DH], wgu[0], LAST, preferred_element_type=F32)
        part = part + lax.dot_general(rows[:, DH:DC], wgu[1], LAST, preferred_element_type=F32)
        if k == 0:
            own[...] = part
        else:
            ps[k - 1] = part.astype(BF)
            p_cp[k] = go(rcopy(ps.at[k - 1], pr.at[k - 1], p_ssem.at[k - 1], p_rsem.at[k - 1], xpeer(NX - k)))

    w_in[2].wait()
    w_out[2].wait_recv()
    wd[:, 0:DH] = wd2[0]
    wd[:, DH:DC] = wd2[1]

    both = own[...]
    for k in near_x:
        p_cp[k].wait_recv()
        both = both + pr[k - 1].astype(F32)
    both = jnp.where(scale > 0.0, both * scale, 0.0)
    gate = both[:, 0:U]
    up = both[:, U:2 * U]
    hb[x] = (gate / (1.0 + jnp.exp(-gate)) * up).astype(BF)
    h_cp = {}
    for k in far_x:
        h_cp[k] = go(rcopy(hb.at[x], hb.at[x], h_ssem.at[k - 1], h_rsem.at[k - 1], xpeer(k)))

    for k in [0] + near_x:
        j = lax.rem(x - k + NX, NX)
        if k:
            h_cp[k].wait_recv()
        part = jnp.dot(hb[j], wd[...], preferred_element_type=F32).astype(BF)
        for half in range(2):
            for e in range(E):
                q = half * E + e
                bs[half, j * E + e] = part[q * GR:(q + 1) * GR]
    b1_cp = {}
    for k in far_y:
        for half in range(2):
            g = lax.rem(here[half] + k, NG)
            b1_cp[half, k] = go(rcopy(
                bs.at[half, g], r1.at[half, k - 1], b1_ssem.at[half, k - 1], b1_rsem.at[half, k - 1], first[half](k)
            ))
    b2_cp = {}
    for half in range(2):
        total = bs[half, here[half]].astype(F32)
        for k in near_first(NY):
            b1_cp[half, k].wait_recv()
            total = total + r1[half, k - 1].astype(F32)
        s1[half] = total.astype(BF)
        for k in far_y:
            b2_cp[half, k] = go(rcopy(
                s1.at[half], r2.at[half, k - 1], b2_ssem.at[half, k - 1], b2_rsem.at[half, k - 1], second[half](k)
            ))

    gain_post = gain(1)
    gain_final = gain(2)
    lane = lax.broadcasted_iota(jnp.int32, (GR, 128), 1)
    halves = []
    for half in range(2):
        branch = s1[half].astype(F32)
        for k in near_first(NY):
            b2_cp[half, k].wait_recv()
            branch = branch + r2[half, k - 1].astype(F32)
        rows = hx[here[half] // E, half * E + here[half] % E].astype(F32)
        scaled = branch * gain_post
        sums = jnp.where(lane == 0, jnp.sum(branch * branch, axis=1, keepdims=True), 0.0)
        sums = jnp.where(lane == 1, jnp.sum(rows * scaled, axis=1, keepdims=True), sums)
        sums = jnp.where(lane == 2, jnp.sum(scaled * scaled, axis=1, keepdims=True), sums)
        sums = jnp.where(lane == 3, jnp.sum(rows * rows, axis=1, keepdims=True), sums)
        st[half] = sums
        halves.append((rows, scaled))
    n_cp = {}
    for k in far_x:
        n_cp[k] = go(rcopy(st, sr.at[k - 1], n_ssem.at[k - 1], n_rsem.at[k - 1], xpeer(k)))
    all_sums = [st[half] for half in range(2)]
    for k in near_x:
        n_cp[k].wait_recv()
        all_sums = [all_sums[half] + sr[k - 1, half] for half in range(2)]
    ga_cp = {}
    gb_cp = {}
    for half in range(2):
        sums = all_sums[half]
        rows, scaled = halves[half]
        factor = lax.rsqrt(sums[:, 0:1] / D + EPS)
        spread = sums[:, 3:4] + factor * (2.0 * sums[:, 1:2] + factor * sums[:, 2:3])
        inverse = lax.rsqrt(jnp.maximum(spread, 0.0) / D + EPS)
        final = ((rows + scaled * factor) * inverse * gain_final).astype(BF)
        g = here[half]
        fa[half, g, x] = final[:, 0:DA]
        fb[half, x, g] = final[:, DA:DC]
        for k in far_x:
            ga_cp[half, k] = go(rcopy(
                fa.at[half, g, x], fa.at[half, g, x], ga_ssem.at[half, k - 1], ga_rsem.at[half, k - 1], xpeer(k)
            ))
        for k in far_y:
            gb_cp[half, k] = go(rcopy(
                fb.at[half, x, g], fb.at[half, x, g], gb_ssem.at[half, k - 1], gb_rsem.at[half, k - 1], first[half](k)
            ))

    rings = {}

    def ring(half, s):
        g = here[half]
        up_g = lax.rem(g - s + NG, NG)
        down_g = lax.rem(g + s, NG)
        if s < NG // 2 - 1:
            a = (fa.at[half, up_g], fa.at[half, down_g])
        else:
            a = (fa.at[half, up_g, 0:NX // 2], fa.at[half, down_g, NX // 2:NX])
        rings[half, s] = (
            go(rcopy(a[0], a[0], rr_ssem.at[half, s], rr_rsem.at[half, s], first[half](1))),
            go(rcopy(a[1], a[1], rl_ssem.at[half, s], rl_rsem.at[half, s], first[half](NG - 1))),
        )

    def ring_wait(half, s):
        for cp in rings[half, s]:
            cp.wait_recv()

    for half in range(2):
        for k in near_x:
            ga_cp[half, k].wait_recv()
        ring(half, 0)
    gx_cp = {}
    for half in range(2):
        for k in near_first(NY):
            gb_cp[half, k].wait_recv()
        for k in far_x:
            gx_cp[half, k] = go(rcopy(
                fb.at[half, x], fb.at[half, x], gx_ssem.at[half, k - 1], gx_rsem.at[half, k - 1], xpeer(k)
            ))
    for s in range(1, NG // 2):
        for half in range(2):
            ring_wait(half, s - 1)
            ring(half, s)

    w_in[3].wait()
    w_out[3].wait_recv()
    for k in range(1, NX):
        t_cp[k].wait_recv()
    tok_cols = [jnp.sum(jnp.where(eye_low, tk[j, 0:1], 0.0), axis=1, keepdims=True) for j in range(NX)]
    HR = LIVE // 2
    entry = lax.broadcasted_iota(jnp.int32, (NG * GR, VS), 1).astype(F32)
    totals = []
    targets = []
    for half in range(2):
        ring_wait(half, NG // 2 - 1)
        for k in near_x:
            gx_cp[half, k].wait_recv()
        tok_half = jnp.concatenate([t[half * HR:(half + 1) * HR] for t in tok_cols], axis=0)
        total = jnp.zeros((NG * GR, 1), F32)
        target = jnp.zeros((NG * GR, 1), F32)
        for which in range(2):
            logits = jnp.zeros((NG * GR, VS), F32)
            for j in range(NX):
                logits = logits + jnp.dot(
                    fa[half, :, j].reshape(NG * GR, DA), un[which, j * DC:j * DC + DA], preferred_element_type=F32
                )
                logits = logits + jnp.dot(
                    fb[half, j].reshape(NG * GR, DC - DA), un[which, j * DC + DA:(j + 1) * DC], preferred_element_type=F32
                )
            capped = CAP * jnp.tanh(logits / CAP)
            offset = (((x * 2 + which) * NZ + z) * NY + y) * VS
            total = total + jnp.sum(jnp.exp(capped - CAP), axis=1, keepdims=True)
            target = target + jnp.sum(
                jnp.where(entry == tok_half - offset.astype(F32), capped, 0.0), axis=1, keepdims=True
            )
        totals.append(total)
        targets.append(target)

    for j in range(NX):
        t = jnp.concatenate([v[j * HR:(j + 1) * HR] for v in totals], axis=0)
        g = jnp.concatenate([v[j * HR:(j + 1) * HR] for v in targets], axis=0)
        row = jnp.sum(jnp.where(eye_low, t, 0.0) + jnp.where(eye_high, g, 0.0), axis=0, keepdims=True)
        fs[j] = jnp.broadcast_to(row, (8, TOK))
    fx_cp = {}
    for k in far_x:
        fx_cp[k] = go(rcopy(fs.at[lax.rem(x + k, NX)], fx.at[k - 1], fx_ssem.at[k - 1], fx_rsem.at[k - 1], xpeer(k)))
    acc = fs[x]
    for k in near_x:
        fx_cp[k].wait_recv()
        acc = acc + fx[k - 1]
    fyb[...] = acc
    fy_cp = {}
    for k in far_y:
        fy_cp[k] = go(rcopy(fyb, fy.at[k - 1], fy_ssem.at[k - 1], fy_rsem.at[k - 1], ypeer(k)))
    for k in near_first(NY):
        fy_cp[k].wait_recv()
        acc = acc + fy[k - 1]
    fzb[...] = acc
    fz_cp = {}
    for k in far_y:
        fz_cp[k] = go(rcopy(fzb, fz.at[k - 1], fz_ssem.at[k - 1], fz_rsem.at[k - 1], zpeer(k)))
    for k in near_first(NY):
        fz_cp[k].wait_recv()
        acc = acc + fz[k - 1]
    row = acc[0:1]
    t = jnp.sum(jnp.where(eye_low, row, 0.0), axis=1, keepdims=True)
    g = jnp.sum(jnp.where(eye_high, row, 0.0), axis=1, keepdims=True)
    logprob = g - CAP - jnp.log(t)
    out_ref[...] = jnp.sum(jnp.where(pick, logprob, 0.0), axis=0, keepdims=True)
    for cp in sent:
        cp.wait_send()


def solution(mesh):
    NX = mesh.shape["dp"] // 2
    NY = mesh.shape["vocab"]
    NZ = mesh.shape["tensor"]

    def on_device(
        hidden_in, norm_pre, w_gate, w_up, w_down, norm_post, norm_final, unembed, token_ids, lengths
    ):
        TOK, D = hidden_in.shape
        U = w_gate.shape[1]
        VS = unembed.shape[1]
        DC = D // NX
        DH = DC // 2
        DA = DC // 3 * 2
        NG = NY
        GR = NX * LIVE // (2 * NG)
        E = NG // NX
        cfg = (NX, NY, NZ, D, U, VS)
        any_spec = pl.BlockSpec(memory_space=pl.ANY)
        vmem = pl.BlockSpec(memory_space=pltpu.VMEM)
        dma = lambda *s: pltpu.SemaphoreType.DMA(s)
        xs = NX - 1
        ys = NY - 1
        pairs = lambda *s: [dma(*s), dma(*s)]
        lines = lambda v: v.reshape(D // 128, 128)
        out = pl.pallas_call(
            functools.partial(kernel, cfg),
            out_shape=jax.ShapeDtypeStruct((1, TOK), F32),
            in_specs=[any_spec] * 10,
            out_specs=vmem,
            scratch_shapes=[
                pltpu.VMEM((TOK, D), BF),
                pltpu.VMEM((3, D // 128, 128), F32),
                pltpu.VMEM((1, TOK), jnp.int32),
                pltpu.SMEM((2,), jnp.int32),
                pltpu.VMEM((xs, 2 * E, GR, DC), BF),
                pltpu.VMEM((NX, 2 * E, GR, DC), BF),
                pltpu.VMEM((2, 2 * U, DH), BF),
                pltpu.VMEM((2, U, DH), BF),
                pltpu.VMEM((U, DC), BF),
                pltpu.VMEM((2, D, VS), BF),
                pltpu.VMEM((LIVE, 2 * U), F32),
                pltpu.VMEM((xs, LIVE, 2 * U), BF),
                pltpu.VMEM((xs, LIVE, 2 * U), BF),
                pltpu.VMEM((NX, LIVE, U), BF),
                pltpu.VMEM((2, NG, GR, DC), BF),
                pltpu.VMEM((2, ys, GR, DC), BF),
                pltpu.VMEM((2, GR, DC), BF),
                pltpu.VMEM((2, ys, GR, DC), BF),
                pltpu.VMEM((2, GR, 128), F32),
                pltpu.VMEM((xs, 2, GR, 128), F32),
                pltpu.VMEM((2, NG, NX, GR, DA), BF),
                pltpu.VMEM((2, NX, NG, GR, DC - DA), BF),
                pltpu.VMEM((NX, 8, TOK), F32),
                pltpu.VMEM((NX, 8, TOK), F32),
                pltpu.VMEM((xs, 8, TOK), F32),
                pltpu.VMEM((8, TOK), F32),
                pltpu.VMEM((ys, 8, TOK), F32),
                pltpu.VMEM((8, TOK), F32),
                pltpu.VMEM((ys, 8, TOK), F32),
                dma(NX + 9),
            ]
            + pairs(4) + pairs(xs) + pairs(xs) + pairs(xs) + pairs(xs)
            + pairs(2, ys) + pairs(2, ys) + pairs(xs) + pairs(2, xs) + pairs(2, ys)
            + pairs(2, NG // 2) + pairs(2, NG // 2) + pairs(2, xs) + pairs(xs) + pairs(ys) + pairs(ys),
            compiler_params=pltpu.CompilerParams(
                collective_id=0, has_side_effects=True, vmem_limit_bytes=60 * 1024 * 1024
            ),
            name="rollout_logprob",
        )(
            hidden_in, lines(norm_pre), lines(norm_post), lines(norm_final), w_gate.T, w_up.T, w_down, unembed,
            token_ids.reshape(1, TOK), lengths,
        )
        return out.reshape(TOK)

    in_specs = (
        P("dp", None),
        P(),
        P("dp", ("tensor", "vocab")),
        P("dp", ("tensor", "vocab")),
        P(("tensor", "vocab"), "dp"),
        P(),
        P(),
        P(None, ("dp", "tensor", "vocab")),
        P("dp"),
        P("dp"),
    )
    return jax.shard_map(
        on_device, mesh=mesh, in_specs=in_specs, out_specs=P("dp"), check_vma=False
    )
```

time: 465 us -> 94.4 us (0.20)
  waiting for transfers between devices: 282 us -> 0 us
  blocking collectives: 131 us -> 0 us
  Pallas kernels: 0 us -> 92.2 us
  local copies, waits for them, and re-layouts: 14.6 us -> 1.19 us
  between operations: 13.3 us -> 0.01 us
  matrix products: 11.7 us -> 0 us
  other arithmetic: 10.1 us -> 0 us
    psum x1 -> x0, waiting for transfers between devices: 166 us -> none  [on_device(): summed = lax.psum(branch, ('tensor', 'vocab'))]
    psum x1 -> x0, blocking collectives: 99.7 us -> none  [on_device(): lax.psum((totals, sampled), ('dp', 'tensor', 'vocab'))]
    pallas_call x0 -> x1, Pallas kernels: none -> 92.2 us  [on_device(): pl.pallas_call(functools.partial(kernel, cfg), out_shape=jax.ShapeDtypeSt...]
    all_gather x2 -> x0, waiting for transfers between devices: 81.3 us -> none  [the longest x1 46.7 us: on_device(): lax.all_gather(final, 'dp', axis=0, tiled=True)]
    unnamed x5 -> x0, waiting for transfers between devices: 35.2 us -> none
    all_to_all x1 -> x0, blocking collectives: 23.8 us -> none  [on_device(): lax.all_to_all(normed, 'dp', split_axis=1, concat_axis=0, tiled=True)]
    dot_general x3 -> x0, matrix products: 11.7 us -> none  [the longest x1 6.58 us: on_device(): jnp.dot(every_row, unembed, preferred_element_type=jnp.float32) / CAP]
    all_gather x1 -> x0, blocking collectives: 7.38 us -> none  [on_device(): lax.all_gather(token_ids, 'dp', axis=0, tiled=True)]
  transfers between devices with their start and end apart: 4 -> 0, of which waited for: 4 -> 0; matrix products, arithmetic and copies ran while one was open for 0% -> 0% of each run, Pallas kernels for 0% -> 0%
where the time goes in v1:
time: 94.4 us; the launch traced here: 93.4 us
  Pallas kernels  92.2 us (98%)
  local copies, waits for them, and re-layouts  1.19 us (1%)
    pallas_call x1, Pallas kernels, on_device(): pl.pallas_call(functools.partial(kernel, cfg), out_shape=jax.ShapeDtypeSt...  92.2 us

profile of v1, /device:TPU:6, one launch (start us, length us, event | category | flops | bytes accessed | tf_op | source)
XLA Modules:
  0.0 93.4 jit_solution(16632982647294724668)
XLA Ops:
  0.0 92.2 %rollout_logprob.1 = f32[1,128]{1,0:T(1,128)} custom-call(bf16[128,4608]{1,0:T(8,128)(2,1)} %hid_hbm.1, f32[36,128]{1,0:T(8,128)} %bitcast.9, f32[36,128]{1,0:T(8,128)} %bitcast.10, f32[36,128]{1,0:T(8,128)} %bitcast.11, bf16[288,576]{1,0:T(8,128)(2,1)} %bitcast.7, bf16[288,576]{1,0:T(8,128)(2,1)} %bitcast.8, bf16[288,576]{1,0:T(8,128)(2,1)} %wd_hbm.1, ...), custom_call_target="tpu_custom_call" | custom-call | tf_op jit(solution)/shard_map/rollout_logprob/pallas_call | solution.py:407
  92.2 1.2 %copy.12 = f32[128]{0:T(128)} copy(f32[128]{0:T(128)} %bitcast.13) | data formatting | bytes 1024

commit v2 on v1

--- a/solution.py
+++ b/solution.py
@@ -9,6 +9,8 @@
 
 EPS = 1e-06
 CAP = 30.0
+HOPS = (0, 1, 2, 3)
+PIECES = 4
 LIVE = 64
 MESH = pl.DeviceIdType.MESH
 BF = jnp.bfloat16
@@ -34,10 +36,10 @@
     hid_hbm, pre_hbm, post_hbm, fin_hbm, wg_hbm, wu_hbm, wd_hbm, un_hbm, tok_hbm, len_hbm,
     out_ref,
     hid, gains, tok_ref, len_ref, hs, hx, wgu, wd2, wd, un,
-    own, ps, pr, hb, bs, r1, s1, r2, st, sr, fa, fb, tk, fs, fx, fyb, fy, fzb, fz,
+    own, ps, pr, hb, bs, r1, s1, r2, hrow, bx, flow, fa, lg, tk, fs, fx, fyb, fy, fzb, fz,
     l_sem, c_ssem, c_rsem, a_ssem, a_rsem, t_ssem, t_rsem, p_ssem, p_rsem, h_ssem, h_rsem,
-    b1_ssem, b1_rsem, b2_ssem, b2_rsem, n_ssem, n_rsem, ga_ssem, ga_rsem, gb_ssem, gb_rsem,
-    rr_ssem, rr_rsem, rl_ssem, rl_rsem, gx_ssem, gx_rsem, fx_ssem, fx_rsem, fy_ssem, fy_rsem, fz_ssem, fz_rsem,
+    b1_ssem, b1_rsem, b2_ssem, b2_rsem, n_ssem, n_rsem, q_ssem, q_rsem,
+    rr_ssem, rr_rsem, fx_ssem, fx_rsem, fy_ssem, fy_rsem, fz_ssem, fz_rsem,
 ):
     NX, NY, NZ, D, U, VS = cfg
     DC = D // NX
@@ -45,7 +47,6 @@
     NG = NY
     E = NG // NX
     GR = NX * LIVE // (2 * NG)
-    DA = fa.shape[-1]
     TOK = hid.shape[0]
     dp = lax.axis_index("dp")
     z = lax.axis_index("tensor")
@@ -74,6 +75,10 @@
 
     sent = []
 
+    def drain(keep=0):
+        while len(sent) > keep:
+            sent.pop(0).wait_send()
+
     def go(copy):
         copy.start()
         sent.append(copy)
@@ -83,16 +88,21 @@
     near_x = near_first(NX)
     far_y = far_first(NY)
 
+    barrier = pltpu.get_barrier_semaphore()
+    partners = [core] + [xpeer(k) for k in range(1, NX)] + [ypeer(k) for k in range(1, NY)] + [zpeer(k) for k in range(1, NZ)]
+    for dev in partners:
+        pl.semaphore_signal(barrier, inc=1, device_id=dev, device_id_type=MESH)
+
     tok_in = pltpu.make_async_copy(tok_hbm, tok_ref, l_sem.at[NX + 7])
     len_in = pltpu.make_async_copy(len_hbm, len_ref, l_sem.at[NX + 8])
     len_in.start()
-    tok_in.start()
     hid_in = []
     for n, k in enumerate(far_x + [0]):
         cols = pl.ds(pl.multiple_of(lax.rem(x + k, NX) * DC, 128), DC)
         cp = pltpu.make_async_copy(hid_hbm.at[:, cols], hid.at[:, cols], l_sem.at[n])
         cp.start()
         hid_in.append((k, cols, cp))
+    tok_in.start()
     w_in = [
         pltpu.make_async_copy(wg_hbm, wgu.at[c, 0:U], l_sem.at[NX]),
         pltpu.make_async_copy(wu_hbm, wgu.at[c, U:2 * U], l_sem.at[NX + 1]),
@@ -107,15 +117,9 @@
         cp.start()
         gain_in.append(cp)
 
-    def gain(n):
-        gain_in[n].wait()
+    def gain(n, j):
         lines = DC // 128
-        return jnp.concatenate([gains[n, pl.ds(x * lines + i, 1)] for i in range(lines)], axis=1)
-
-    barrier = pltpu.get_barrier_semaphore()
-    partners = [core] + [xpeer(k) for k in range(1, NX)] + [ypeer(k) for k in range(1, NY)] + [zpeer(k) for k in range(1, NZ)]
-    for dev in partners:
-        pl.semaphore_signal(barrier, inc=1, device_id=dev, device_id_type=MESH)
+        return jnp.concatenate([gains[n, pl.ds(j * lines + i, 1)] for i in range(lines)], axis=1)
 
     len_in.wait()
     l0 = len_ref[0]
@@ -165,7 +169,8 @@
     for k in range(1, NX):
         t_cp[k] = go(rcopy(tk.at[x], tk.at[x], t_ssem.at[k - 1], t_rsem.at[k - 1], xpeer(k)))
 
-    gain_pre = gain(0)
+    gain_in[0].wait()
+    gain_pre = gain(0, x)
     for n in range(2):
         w_in[n].wait()
         w_out[n].wait_recv()
@@ -201,6 +206,13 @@
     for k in far_x:
         h_cp[k] = go(rcopy(hb.at[x], hb.at[x], h_ssem.at[k - 1], h_rsem.at[k - 1], xpeer(k)))
 
+    b1_cp = {}
+    for half in range(2):
+        for k in far_y:
+            g = lax.rem(here[half] + k, NG)
+            b1_cp[half, k] = rcopy(
+                bs.at[half, g], r1.at[half, k - 1], b1_ssem.at[half, k - 1], b1_rsem.at[half, k - 1], first[half](k)
+            )
     for k in [0] + near_x:
         j = lax.rem(x - k + NX, NX)
         if k:
@@ -209,14 +221,30 @@
         for half in range(2):
             for e in range(E):
                 q = half * E + e
-                bs[half, j * E + e] = part[q * GR:(q + 1) * GR]
-    b1_cp = {}
-    for k in far_y:
+                bs[half, e * NX + j] = part[q * GR:(q + 1) * GR]
         for half in range(2):
-            g = lax.rem(here[half] + k, NG)
-            b1_cp[half, k] = go(rcopy(
-                bs.at[half, g], r1.at[half, k - 1], b1_ssem.at[half, k - 1], b1_rsem.at[half, k - 1], first[half](k)
-            ))
+            for e in range(E):
+                away = lax.rem(e * NX + j - here[half] + NG, NG)
+
+                @pl.when(away > 0)
+                def _(half=half, g=e * NX + j, away=away):
+                    rcopy(
+                        bs.at[half, g], r1.at[half, away - 1], b1_ssem.at[half, away - 1], b1_rsem.at[half, away - 1],
+                        {"vocab": g} if half == 0 else {"tensor": g},
+                    ).start()
+    sent.extend(b1_cp[half, k] for half in range(2) for k in far_y)
+    for half in range(2):
+        q = half * E + here[half] // NX
+
+        @pl.when(x == lax.rem(here[half], NX))
+        def _(half=half, q=q):
+            hrow[half, x] = hx[x, q]
+            for k in range(1, NX):
+                hrow[half, lax.rem(x + k, NX)] = hs[k - 1, q]
+            for k in far_x:
+                rcopy(hrow.at[half], hrow.at[half], q_ssem.at[half, k - 1], q_rsem.at[half], xpeer(k)).start()
+
+    drain(keep=14)
     b2_cp = {}
     for half in range(2):
         total = bs[half, here[half]].astype(F32)
@@ -229,112 +257,120 @@
                 s1.at[half], r2.at[half, k - 1], b2_ssem.at[half, k - 1], b2_rsem.at[half, k - 1], second[half](k)
             ))
 
-    gain_post = gain(1)
-    gain_final = gain(2)
-    lane = lax.broadcasted_iota(jnp.int32, (GR, 128), 1)
-    halves = []
+    drain(keep=14)
+    bx_cp = {}
     for half in range(2):
         branch = s1[half].astype(F32)
         for k in near_first(NY):
             b2_cp[half, k].wait_recv()
             branch = branch + r2[half, k - 1].astype(F32)
-        rows = hx[here[half] // E, half * E + here[half] % E].astype(F32)
-        scaled = branch * gain_post
-        sums = jnp.where(lane == 0, jnp.sum(branch * branch, axis=1, keepdims=True), 0.0)
-        sums = jnp.where(lane == 1, jnp.sum(rows * scaled, axis=1, keepdims=True), sums)
-        sums = jnp.where(lane == 2, jnp.sum(scaled * scaled, axis=1, keepdims=True), sums)
-        sums = jnp.where(lane == 3, jnp.sum(rows * rows, axis=1, keepdims=True), sums)
-        st[half] = sums
-        halves.append((rows, scaled))
-    n_cp = {}
-    for k in far_x:
-        n_cp[k] = go(rcopy(st, sr.at[k - 1], n_ssem.at[k - 1], n_rsem.at[k - 1], xpeer(k)))
-    all_sums = [st[half] for half in range(2)]
-    for k in near_x:
-        n_cp[k].wait_recv()
-        all_sums = [all_sums[half] + sr[k - 1, half] for half in range(2)]
-    ga_cp = {}
-    gb_cp = {}
-    for half in range(2):
-        sums = all_sums[half]
-        rows, scaled = halves[half]
-        factor = lax.rsqrt(sums[:, 0:1] / D + EPS)
-        spread = sums[:, 3:4] + factor * (2.0 * sums[:, 1:2] + factor * sums[:, 2:3])
-        inverse = lax.rsqrt(jnp.maximum(spread, 0.0) / D + EPS)
-        final = ((rows + scaled * factor) * inverse * gain_final).astype(BF)
-        g = here[half]
-        fa[half, g, x] = final[:, 0:DA]
-        fb[half, x, g] = final[:, DA:DC]
+        bx[half, x] = branch.astype(BF)
         for k in far_x:
-            ga_cp[half, k] = go(rcopy(
-                fa.at[half, g, x], fa.at[half, g, x], ga_ssem.at[half, k - 1], ga_rsem.at[half, k - 1], xpeer(k)
+            bx_cp[half, k] = go(rcopy(
+                bx.at[half, x], bx.at[half, x], n_ssem.at[half, k - 1], n_rsem.at[half, k - 1], xpeer(k)
             ))
-        for k in far_y:
-            gb_cp[half, k] = go(rcopy(
-                fb.at[half, x, g], fb.at[half, x, g], gb_ssem.at[half, k - 1], gb_rsem.at[half, k - 1], first[half](k)
-            ))
-
+    gain_in[1].wait()
+    gain_in[2].wait()
+    for half in range(2):
+        whole = rcopy(hrow.at[half], hrow.at[half], q_ssem.at[half, 0], q_rsem.at[half], xpeer(1))
+
+        @pl.when(x != lax.rem(here[half], NX))
+        def _(whole=whole):
+            whole.wait_recv()
+
+        @pl.when(x == lax.rem(here[half], NX))
+        def _(half=half):
+            for k in far_x:
+                rcopy(hrow.at[half], hrow.at[half], q_ssem.at[half, k - 1], q_rsem.at[half], xpeer(k)).wait_send()
+
+    for half in range(2):
+        for k in near_x:
+            bx_cp[half, k].wait_recv()
+        branches = [bx[half, j].astype(F32) for j in range(NX)]
+        square = sum(jnp.sum(b * b, axis=1, keepdims=True) for b in branches)
+        factor = lax.rsqrt(square / D + EPS)
+        square = jnp.zeros((GR, 1), F32)
+        for j in range(NX):
+            stream = hrow[half, j].astype(F32) + branches[j] * factor * gain(1, j)
+            flow[half, j] = stream
+            square = square + jnp.sum(stream * stream, axis=1, keepdims=True)
+        inverse = lax.rsqrt(square / D + EPS)
+        for j in range(NX):
+            fa[half, here[half], j] = (flow[half, j] * inverse * gain(2, j)).astype(BF)
+
+    last = NG // 2 - 1
+    source = HOPS
+    pieces = PIECES
+    width = NX // pieces
     rings = {}
-
-    def ring(half, s):
-        g = here[half]
-        up_g = lax.rem(g - s + NG, NG)
-        down_g = lax.rem(g + s, NG)
-        if s < NG // 2 - 1:
-            a = (fa.at[half, up_g], fa.at[half, down_g])
-        else:
-            a = (fa.at[half, up_g, 0:NX // 2], fa.at[half, down_g, NX // 2:NX])
-        rings[half, s] = (
-            go(rcopy(a[0], a[0], rr_ssem.at[half, s], rr_rsem.at[half, s], first[half](1))),
-            go(rcopy(a[1], a[1], rl_ssem.at[half, s], rl_rsem.at[half, s], first[half](NG - 1))),
-        )
-
-    def ring_wait(half, s):
-        for cp in rings[half, s]:
-            cp.wait_recv()
-
-    for half in range(2):
-        for k in near_x:
-            ga_cp[half, k].wait_recv()
-        ring(half, 0)
-    gx_cp = {}
-    for half in range(2):
-        for k in near_first(NY):
-            gb_cp[half, k].wait_recv()
-        for k in far_x:
-            gx_cp[half, k] = go(rcopy(
-                fb.at[half, x], fb.at[half, x], gx_ssem.at[half, k - 1], gx_rsem.at[half, k - 1], xpeer(k)
-            ))
-    for s in range(1, NG // 2):
+    got = set()
+
+    def arrived(*key):
+        if key not in got:
+            got.add(key)
+            rings[key].wait_recv()
+
+    def runs(s, i, way):
+        return s < last or (i < pieces // 2) == (way == 0)
+
+    def ring(s, i):
+        near = source[s]
         for half in range(2):
-            ring_wait(half, s - 1)
-            ring(half, s)
-
-    w_in[3].wait()
-    w_out[3].wait_recv()
+            for way in range(2):
+                if near:
+                    arrived(half, near - 1, i, way)
+                if runs(s, i, way):
+                    block = fa.at[half, lax.rem(here[half] + (near if way else NG - near), NG), pl.ds(i * width, width)]
+                    hops = s + 1 - near
+                    rings[half, s, i, way] = go(rcopy(
+                        block, block, rr_ssem.at[half, s, i, way], rr_rsem.at[half, s, i, way],
+                        first[half](NG - hops if way else hops)
+                    ))
+
+    def multiply(shifts):
+        picks = []
+        for half in range(2):
+            for shift in shifts:
+                for i in range(pieces):
+                    for way in range(2):
+                        if shift and runs(shift - 1, i, way):
+                            arrived(half, shift - 1, i, way)
+                for sign in sorted({shift % NG, -shift % NG}):
+                    picks.append((half, lax.rem(here[half] + sign, NG)))
+        lhs = [jnp.concatenate([fa[h, g, j] for h, g in picks], axis=0) for j in range(NX)]
+        for which in range(2):
+            total = jnp.dot(lhs[0], un[which, 0:DC], preferred_element_type=F32)
+            for j in range(1, NX):
+                total = total + jnp.dot(lhs[j], un[which, j * DC:(j + 1) * DC], preferred_element_type=F32)
+            for n, (h, g) in enumerate(picks):
+                lg[which, h, g] = total[n * GR:(n + 1) * GR]
+
+    for s in range(NG // 2):
+        for i in range(pieces):
+            ring(s, i)
+        if s == 0:
+            w_in[3].wait()
+            w_out[3].wait_recv()
     for k in range(1, NX):
         t_cp[k].wait_recv()
     tok_cols = [jnp.sum(jnp.where(eye_low, tk[j, 0:1], 0.0), axis=1, keepdims=True) for j in range(NX)]
+    multiply([0, 1] if last > 0 else [0])
+    drain(keep=40)
+    for s in range(2, NG // 2):
+        multiply([s])
+    multiply([NG // 2])
     HR = LIVE // 2
     entry = lax.broadcasted_iota(jnp.int32, (NG * GR, VS), 1).astype(F32)
     totals = []
     targets = []
     for half in range(2):
-        ring_wait(half, NG // 2 - 1)
-        for k in near_x:
-            gx_cp[half, k].wait_recv()
-        tok_half = jnp.concatenate([t[half * HR:(half + 1) * HR] for t in tok_cols], axis=0)
+        tok_half = jnp.concatenate(
+            [t[half * HR + e * GR:half * HR + (e + 1) * GR] for e in range(E) for t in tok_cols], axis=0
+        )
         total = jnp.zeros((NG * GR, 1), F32)
         target = jnp.zeros((NG * GR, 1), F32)
         for which in range(2):
-            logits = jnp.zeros((NG * GR, VS), F32)
-            for j in range(NX):
-                logits = logits + jnp.dot(
-                    fa[half, :, j].reshape(NG * GR, DA), un[which, j * DC:j * DC + DA], preferred_element_type=F32
-                )
-                logits = logits + jnp.dot(
-                    fb[half, j].reshape(NG * GR, DC - DA), un[which, j * DC + DA:(j + 1) * DC], preferred_element_type=F32
-                )
+            logits = lg[which, half].reshape(NG * GR, VS)
             capped = CAP * jnp.tanh(logits / CAP)
             offset = (((x * 2 + which) * NZ + z) * NY + y) * VS
             total = total + jnp.sum(jnp.exp(capped - CAP), axis=1, keepdims=True)
@@ -345,8 +381,9 @@
         targets.append(target)
 
     for j in range(NX):
-        t = jnp.concatenate([v[j * HR:(j + 1) * HR] for v in totals], axis=0)
-        g = jnp.concatenate([v[j * HR:(j + 1) * HR] for v in targets], axis=0)
+        spans = [(half, (e * NX + j) * GR) for half in range(2) for e in range(E)]
+        t = jnp.concatenate([totals[half][at:at + GR] for half, at in spans], axis=0)
+        g = jnp.concatenate([targets[half][at:at + GR] for half, at in spans], axis=0)
         row = jnp.sum(jnp.where(eye_low, t, 0.0) + jnp.where(eye_high, g, 0.0), axis=0, keepdims=True)
         fs[j] = jnp.broadcast_to(row, (8, TOK))
     fx_cp = {}
@@ -356,6 +393,7 @@
     for k in near_x:
         fx_cp[k].wait_recv()
         acc = acc + fx[k - 1]
+    drain(keep=3)
     fyb[...] = acc
     fy_cp = {}
     for k in far_y:
@@ -375,8 +413,7 @@
     g = jnp.sum(jnp.where(eye_high, row, 0.0), axis=1, keepdims=True)
     logprob = g - CAP - jnp.log(t)
     out_ref[...] = jnp.sum(jnp.where(pick, logprob, 0.0), axis=0, keepdims=True)
-    for cp in sent:
-        cp.wait_send()
+    drain()
 
 
 def solution(mesh):
@@ -392,7 +429,6 @@
         VS = unembed.shape[1]
         DC = D // NX
         DH = DC // 2
-        DA = DC // 3 * 2
         NG = NY
         GR = NX * LIVE // (2 * NG)
         E = NG // NX
@@ -428,10 +464,11 @@
                 pltpu.VMEM((2, ys, GR, DC), BF),
                 pltpu.VMEM((2, GR, DC), BF),
                 pltpu.VMEM((2, ys, GR, DC), BF),
-                pltpu.VMEM((2, GR, 128), F32),
-                pltpu.VMEM((xs, 2, GR, 128), F32),
-                pltpu.VMEM((2, NG, NX, GR, DA), BF),
-                pltpu.VMEM((2, NX, NG, GR, DC - DA), BF),
+                pltpu.VMEM((2, NX, GR, DC), BF),
+                pltpu.VMEM((2, NX, GR, DC), BF),
+                pltpu.VMEM((2, NX, GR, DC), F32),
+                pltpu.VMEM((2, NG, NX, GR, DC), BF),
+                pltpu.VMEM((2, 2, NG, GR, VS), F32),
                 pltpu.VMEM((NX, 8, TOK), F32),
                 pltpu.VMEM((NX, 8, TOK), F32),
                 pltpu.VMEM((xs, 8, TOK), F32),
@@ -442,8 +479,8 @@
                 dma(NX + 9),
             ]
             + pairs(4) + pairs(xs) + pairs(xs) + pairs(xs) + pairs(xs)
-            + pairs(2, ys) + pairs(2, ys) + pairs(xs) + pairs(2, xs) + pairs(2, ys)
-            + pairs(2, NG // 2) + pairs(2, NG // 2) + pairs(2, xs) + pairs(xs) + pairs(ys) + pairs(ys),
+            + pairs(2, ys) + pairs(2, ys) + pairs(2, xs) + [dma(2, xs), dma(2)]
+            + pairs(2, NG // 2, NX, 2) + pairs(xs) + pairs(ys) + pairs(ys),
             compiler_params=pltpu.CompilerParams(
                 collective_id=0, has_side_effects=True, vmem_limit_bytes=60 * 1024 * 1024
             ),

time: 94.4 us -> 89.7 us (0.950)
  Pallas kernels: 92.2 us -> 88.3 us
    pallas_call x1, Pallas kernels: 92.2 us -> 88.3 us  [on_device(): pl.pallas_call(functools.partial(kernel, cfg), out_shape=jax.ShapeDtypeSt...]
where the time goes in v2:
time: 89.7 us; the launch traced here: 89.5 us
  Pallas kernels  88.3 us (98%)
  local copies, waits for them, and re-layouts  1.19 us (1%)
    pallas_call x1, Pallas kernels, on_device(): pl.pallas_call(functools.partial(kernel, cfg), out_shape=jax.ShapeDtypeSt...  88.3 us

profile of v2, /device:TPU:6, one launch (start us, length us, event | category | flops | bytes accessed | tf_op | source)
XLA Modules:
  0.0 89.5 jit_solution(12499079634973859054)
XLA Ops:
  0.0 88.3 %rollout_logprob.1 = f32[1,128]{1,0:T(1,128)} custom-call(bf16[128,4608]{1,0:T(8,128)(2,1)} %hid_hbm.1, f32[36,128]{1,0:T(8,128)} %bitcast.9, f32[36,128]{1,0:T(8,128)} %bitcast.10, f32[36,128]{1,0:T(8,128)} %bitcast.11, bf16[288,576]{1,0:T(8,128)(2,1)} %bitcast.7, bf16[288,576]{1,0:T(8,128)(2,1)} %bitcast.8, bf16[288,576]{1,0:T(8,128)(2,1)} %wd_hbm.1, ...), custom_call_target="tpu_custom_call" | custom-call | tf_op jit(solution)/shard_map/rollout_logprob/pallas_call | solution.py:443
  88.3 1.2 %copy.12 = f32[128]{0:T(128)} copy(f32[128]{0:T(128)} %bitcast.13) | data formatting | bytes 1024

commit v3 on v2

--- a/solution.py
+++ b/solution.py
@@ -175,19 +175,22 @@
         w_in[n].wait()
         w_out[n].wait_recv()
     p_cp = {}
-    for k in [0] + near_x:
-        j = lax.rem(x - k + NX, NX)
-        if k:
-            a_cp[k].wait_recv()
-        rows = hx[j].reshape(LIVE, DC).astype(F32)
-        rows = (rows * gain_pre).astype(BF)
+    batches = [[0], [1, NX - 1], [2]] if NX == 4 else [[k] for k in [0] + near_x]
+    for batch in batches:
+        rows = []
+        for k in batch:
+            if k:
+                a_cp[k].wait_recv()
+            rows.append(hx[lax.rem(x - k + NX, NX)].reshape(LIVE, DC).astype(F32))
+        rows = (jnp.concatenate(rows, axis=0) * gain_pre).astype(BF)
         part = lax.dot_general(rows[:, 0:DH], wgu[0], LAST, preferred_element_type=F32)
         part = part + lax.dot_general(rows[:, DH:DC], wgu[1], LAST, preferred_element_type=F32)
-        if k == 0:
-            own[...] = part
-        else:
-            ps[k - 1] = part.astype(BF)
-            p_cp[k] = go(rcopy(ps.at[k - 1], pr.at[k - 1], p_ssem.at[k - 1], p_rsem.at[k - 1], xpeer(NX - k)))
+        for n, k in enumerate(batch):
+            if k == 0:
+                own[...] = part
+            else:
+                ps[k - 1] = part[n * LIVE:(n + 1) * LIVE].astype(BF)
+                p_cp[k] = go(rcopy(ps.at[k - 1], pr.at[k - 1], p_ssem.at[k - 1], p_rsem.at[k - 1], xpeer(NX - k)))
 
     w_in[2].wait()
     w_out[2].wait_recv()
@@ -269,35 +272,6 @@
             bx_cp[half, k] = go(rcopy(
                 bx.at[half, x], bx.at[half, x], n_ssem.at[half, k - 1], n_rsem.at[half, k - 1], xpeer(k)
             ))
-    gain_in[1].wait()
-    gain_in[2].wait()
-    for half in range(2):
-        whole = rcopy(hrow.at[half], hrow.at[half], q_ssem.at[half, 0], q_rsem.at[half], xpeer(1))
-
-        @pl.when(x != lax.rem(here[half], NX))
-        def _(whole=whole):
-            whole.wait_recv()
-
-        @pl.when(x == lax.rem(here[half], NX))
-        def _(half=half):
-            for k in far_x:
-                rcopy(hrow.at[half], hrow.at[half], q_ssem.at[half, k - 1], q_rsem.at[half], xpeer(k)).wait_send()
-
-    for half in range(2):
-        for k in near_x:
-            bx_cp[half, k].wait_recv()
-        branches = [bx[half, j].astype(F32) for j in range(NX)]
-        square = sum(jnp.sum(b * b, axis=1, keepdims=True) for b in branches)
-        factor = lax.rsqrt(square / D + EPS)
-        square = jnp.zeros((GR, 1), F32)
-        for j in range(NX):
-            stream = hrow[half, j].astype(F32) + branches[j] * factor * gain(1, j)
-            flow[half, j] = stream
-            square = square + jnp.sum(stream * stream, axis=1, keepdims=True)
-        inverse = lax.rsqrt(square / D + EPS)
-        for j in range(NX):
-            fa[half, here[half], j] = (flow[half, j] * inverse * gain(2, j)).astype(BF)
-
     last = NG // 2 - 1
     source = HOPS
     pieces = PIECES
@@ -313,9 +287,9 @@
     def runs(s, i, way):
         return s < last or (i < pieces // 2) == (way == 0)
 
-    def ring(s, i):
+    def ring(s, i, halves=(0, 1)):
         near = source[s]
-        for half in range(2):
+        for half in halves:
             for way in range(2):
                 if near:
                     arrived(half, near - 1, i, way)
@@ -345,8 +319,38 @@
             for n, (h, g) in enumerate(picks):
                 lg[which, h, g] = total[n * GR:(n + 1) * GR]
 
+    gain_in[1].wait()
+    gain_in[2].wait()
+    for half in range(2):
+        whole = rcopy(hrow.at[half], hrow.at[half], q_ssem.at[half, 0], q_rsem.at[half], xpeer(1))
+
+        @pl.when(x != lax.rem(here[half], NX))
+        def _(whole=whole):
+            whole.wait_recv()
+
+        @pl.when(x == lax.rem(here[half], NX))
+        def _(half=half):
+            for k in far_x:
+                rcopy(hrow.at[half], hrow.at[half], q_ssem.at[half, k - 1], q_rsem.at[half], xpeer(k)).wait_send()
+
+    for half in range(2):
+        for k in near_x:
+            bx_cp[half, k].wait_recv()
+        branches = [bx[half, j].astype(F32) for j in range(NX)]
+        square = sum(jnp.sum(b * b, axis=1, keepdims=True) for b in branches)
+        factor = lax.rsqrt(square / D + EPS)
+        square = jnp.zeros((GR, 1), F32)
+        for j in range(NX):
+            stream = hrow[half, j].astype(F32) + branches[j] * factor * gain(1, j)
+            flow[half, j] = stream
+            square = square + jnp.sum(stream * stream, axis=1, keepdims=True)
+        inverse = lax.rsqrt(square / D + EPS)
+        for j in range(NX):
+            fa[half, here[half], j] = (flow[half, j] * inverse * gain(2, j)).astype(BF)
+            ring(0, j, (half,))
+
     for s in range(NG // 2):
-        for i in range(pieces):
+        for i in range(pieces if s else 0):
             ring(s, i)
         if s == 0:
             w_in[3].wait()

time: 89.7 us -> 88.9 us (level)
  Pallas kernels: 88.3 us -> 86.7 us
    pallas_call x1, Pallas kernels: 88.3 us -> 86.7 us  [on_device(): pl.pallas_call(functools.partial(kernel, cfg), out_shape=jax.ShapeDtypeSt...]
where the time goes in v3:
time: 88.9 us; the launch traced here: 87.9 us
  Pallas kernels  86.7 us (98%)
  local copies, waits for them, and re-layouts  1.19 us (1%)
    pallas_call x1, Pallas kernels, on_device(): pl.pallas_call(functools.partial(kernel, cfg), out_shape=jax.ShapeDtypeSt...  86.7 us

profile of v3, /device:TPU:6, one launch (start us, length us, event | category | flops | bytes accessed | tf_op | source)
XLA Modules:
  0.0 87.9 jit_solution(3708310602440503945)
XLA Ops:
  0.0 86.7 %rollout_logprob.1 = f32[1,128]{1,0:T(1,128)} custom-call(bf16[128,4608]{1,0:T(8,128)(2,1)} %hid_hbm.1, f32[36,128]{1,0:T(8,128)} %bitcast.9, f32[36,128]{1,0:T(8,128)} %bitcast.10, f32[36,128]{1,0:T(8,128)} %bitcast.11, bf16[288,576]{1,0:T(8,128)(2,1)} %bitcast.7, bf16[288,576]{1,0:T(8,128)(2,1)} %bitcast.8, bf16[288,576]{1,0:T(8,128)(2,1)} %wd_hbm.1, ...), custom_call_target="tpu_custom_call" | custom-call | tf_op jit(solution)/shard_map/rollout_logprob/pallas_call | solution.py:447
  86.7 1.2 %copy.12 = f32[128]{0:T(128)} copy(f32[128]{0:T(128)} %bitcast.13) | data formatting | bytes 1024
